TPU v7x, 32 devices: a whole 2x2x4 slice. The times are simulated.
32 devices in a mesh: copies: 2 (over y), blk: 4 (over x, core), rows: 4 (over z).
Axes of the slice: x: 2, y: 2, z: 4, core: 2. Of those that a mesh axis runs over, the one named last changes fastest.
Arguments:
- activations: bfloat16 [3584, 4096], P(('copies', 'blk'), 'rows'), parts along dimension 0, may hold values from -6 to 6
- out_grads: bfloat16 [3584, 14848], P(('copies', 'blk'), 'rows'), parts along dimension 0, may hold values from -6 to 6
- eigvecs: float32 [4, 4096, 14848], P('blk', 'rows'), may hold values from -0.0007324219 to 0.0007324219
- eigvals: float32 [4], replicated, may hold values from 0.5 to 4
- segment_ids: int32 [3584], P(('copies', 'blk')), parts along dimension 0, may hold values from 0 to 111, never falling along the last dimension, each value on 1 to 64 neighbouring positions
Outputs:
- influence: float32 [224, 4], P('copies'), parts along dimension 0
There are 2 independent parts, one for each index of `copies`. A program takes and returns all parts, laid end to end along the dimension named above; an argument that names none is the same for every part. Nothing has to cross between parts.
Inputs may be any that keep to these rules, and one draw needn't show every extreme that they name: `segment_ids`: never falling along the tokens; each example holds 1 to 64 consecutive tokens, one exactly 64; examples may cross from one index of blk to the next.
All inputs are finite; a program needn't handle non-finite values.
Results may differ from a plain program's by a relative error of at most 0.0029.
Values may be sent and summed in bfloat16 or wider, within the bound.
A program may use at most 384 MiB of HBM per device.

v0:
```python
import jax
import jax.numpy as jnp
from jax import lax
from jax.sharding import PartitionSpec as P

SEG_MEAN = 16


def passed_along(array, axis, by):
    length = lax.axis_size(axis)
    return lax.ppermute(array, axis, [(i, (i + by) % length) for i in range(length)])


def local(activations, out_grads, eigvecs, eigvals, segment_ids):
    tok_rows = activations.shape[0]
    blocks = lax.axis_size("blk")
    mine = lax.axis_index("blk")
    number = eigvals.shape[0]
    examples = tok_rows * blocks // SEG_MEAN
    widened = activations.astype(jnp.float32)
    slab = eigvecs[0].astype(jnp.bfloat16)
    grads = lax.all_gather(out_grads, "rows", axis=1, tiled=True)
    columns = jnp.arange(number, dtype=jnp.int32)

    def score(piece, owner, totals):
        projected = lax.dot_general(
            grads, piece, (((1,), (1,)), ((), ())), preferred_element_type=jnp.float32
        )
        partial_sum = jnp.sum(projected * widened, axis=1)
        picked = (columns == owner).astype(jnp.float32)
        return totals + partial_sum[:, None] * picked[None, :]

    totals = score(slab, mine, jnp.zeros((tok_rows, number), jnp.float32))
    moving = slab
    for step in range(blocks - 1):
        moving = passed_along(moving, "blk", 1)
        totals = score(moving, (mine - step - 1) % blocks, totals)
    member = (segment_ids[:, None] == jnp.arange(examples, dtype=jnp.int32)[None, :]).astype(
        jnp.float32
    )
    full_tokens = lax.psum(totals, "rows")
    local_scores = jnp.dot(member.T, full_tokens, precision=lax.Precision.HIGHEST)
    scores = lax.psum(local_scores, "blk")
    return scores / eigvals[None, :]


def solution(mesh):
    in_specs = (
        P(("copies", "blk"), "rows"),
        P(("copies", "blk"), "rows"),
        P("blk", "rows", None),
        P(),
        P(("copies", "blk")),
    )
    out_specs = P("copies", None)
    return jax.shard_map(local, mesh=mesh, in_specs=in_specs, out_specs=out_specs, check_vma=False)
```

profile of v0, /device:TPU:0, one launch (start us, length us, event | category | flops | bytes accessed | tf_op | source)
XLA Modules:
  0.0 1072.1 jit_solution(8465460904550439288)
XLA Ops:
  6.5 0.0 copy-start.5
  6.5 0.0 all-gather.2.cloned.1.call-start
  6.5 30.5 %convert_bitcast_fusion = bf16[1024,14848]{1,0:T(8,128)(2,1)} fusion(f32[1,1024,14848]{2,1,0:T(8,128)} %param.7), kind=kLoop, calls=%fused_computation | loop fusion | flops 15204352 | bytes 91226112 | tf_op jit(solution)/shard_map/convert_element_type | solution.py:21
  37.0 0.5 collective-permute-start
  37.5 329.3 %collective-permute-done = bf16[1024,14848]{1,0:T(8,128)(2,1)} collective-permute-done((bf16[1024,14848]{1,0:T(8,128)(2,1)}, bf16[1024,14848]{1,0:T(8,128)(2,1)}, u32[]{:S(2)}, u32[]{:S(2)}) %collective-permute-start) | collective-permute-done | bytes 30408736 | tf_op jit(solution)/shard_map/ppermute | solution.py:11
  366.8 0.0 collective-permute-start.1
  366.8 0.0 all-gather.2.cloned.1.call-update
  366.8 329.1 %collective-permute-done.1 = bf16[1024,14848]{1,0:T(8,128)(2,1)} collective-permute-done((bf16[1024,14848]{1,0:T(8,128)(2,1)}, bf16[1024,14848]{1,0:T(8,128)(2,1)}, u32[]{:S(2)}, u32[]{:S(2)}) %collective-permute-start.1) | collective-permute-done | bytes 30408736 | tf_op jit(solution)/shard_map/ppermute | solution.py:11
  695.9 0.0 collective-permute-start.2
  695.9 0.6 compare_convert_fusion.2
  696.5 0.6 compare_convert_fusion
  697.1 0.0 all-gather.2.cloned.1.call-done
  697.1 0.0 copy-done.5
  697.1 20.6 %fusion = f32[448]{0:T(512)S(1)} fusion(bf16[448,1024]{1,0:T(8,128)(2,1)S(1)} %copy-done.5, bf16[448,14848]{1,0:T(8,128)(2,1)} %all-gather.2.cloned.1.call-done, bf16[1024,14848]{1,0:T(8,128)(2,1)} %convert_bitcast_fusion), kind=kOutput, calls=%fused_computation.5 | convolution fusion | flops 13624475648 | bytes 44631808 | tf_op jit(solution)/shard_map/dot_general | solution.py:26
  717.6 20.6 %fusion.1 = f32[448]{0:T(512)S(1)} fusion(bf16[448,1024]{1,0:T(8,128)(2,1)S(1)} %copy-done.5, bf16[448,14848]{1,0:T(8,128)(2,1)} %all-gather.2.cloned.1.call-done, bf16[1024,14848]{1,0:T(8,128)(2,1)} %collective-permute-done), kind=kOutput, calls=%fused_computation.6 | convolution fusion | flops 13624475648 | bytes 44631808 | tf_op jit(solution)/shard_map/dot_general | solution.py:26
  738.2 20.7 %fusion.2 = f32[448]{0:T(512)S(1)} fusion(bf16[448,1024]{1,0:T(8,128)(2,1)S(1)} %copy-done.5, bf16[448,14848]{1,0:T(8,128)(2,1)} %all-gather.2.cloned.1.call-done, bf16[1024,14848]{1,0:T(8,128)(2,1)} %collective-permute-done.1), kind=kOutput, calls=%fused_computation.7 | convolution fusion | flops 13624475648 | bytes 44631808 | tf_op jit(solution)/shard_map/dot_general | solution.py:26
  758.9 0.0 copy-start
  758.9 0.0 copy-start.1
  758.9 0.0 copy-start.2
  758.9 0.0 copy-start.3
  758.9 0.0 copy-start.6
  759.0 0.0 copy-start.4
  759.0 266.1 %collective-permute-done.2 = bf16[1024,14848]{1,0:T(8,128)(2,1)} collective-permute-done((bf16[1024,14848]{1,0:T(8,128)(2,1)}, bf16[1024,14848]{1,0:T(8,128)(2,1)}, u32[]{:S(2)}, u32[]{:S(2)}) %collective-permute-start.2) | collective-permute-done | bytes 30408736 | tf_op jit(solution)/shard_map/ppermute | solution.py:11
  1025.0 20.6 %fusion.3 = f32[448]{0:T(512)S(1)} fusion(bf16[448,1024]{1,0:T(8,128)(2,1)S(1)} %copy-done.5, bf16[448,14848]{1,0:T(8,128)(2,1)} %all-gather.2.cloned.1.call-done, bf16[1024,14848]{1,0:T(8,128)(2,1)} %collective-permute-done.2), kind=kOutput, calls=%fused_computation.8 | convolution fusion | flops 13624475648 | bytes 44631808 | tf_op jit(solution)/shard_map/dot_general | solution.py:26
  1045.6 0.0 copy-done
  1045.6 0.0 copy-done.1
  1045.6 0.0 copy-done.2
  1045.6 0.0 copy-done.3
  1045.6 0.1 multiply_add_fusion
  1045.7 12.9 %psum.14 = f32[448,4]{0,1:T(4,128)S(1)} all-reduce(f32[448,4]{0,1:T(4,128)S(1)} %multiply_add_fusion), channel_id=1, replica_groups=mesh['copies'=2,'blk'=4,'rows'=4] {'rows'}, use_global_device_ids=true, to_apply=%region_4.5 | all-reduce | flops 1792 | bytes 14336 | tf_op jit(solution)/shard_map/psum | solution.py:41
  1058.6 0.0 copy-done.6
  1058.6 0.2 fusion.4
  1058.9 5.7 psum.15
  1064.5 0.0 copy-done.4
  1064.6 0.7 broadcast_divide_fusion
Async XLA Ops:
  6.5 690.5 %copy-start.5 = (bf16[448,1024]{1,0:T(8,128)(2,1)S(1)}, bf16[448,1024]{1,0:T(8,128)(2,1)}, u32[]{:S(2)}) copy-start(bf16[448,1024]{1,0:T(8,128)(2,1)} %param.5) | copy-start | bytes 2752516
  6.5 690.5 %all-gather.2.cloned.1.call-start = ((), (), s32[]{:S(2)}) async-start(), calls=%async_computation | async-start | bytes 16629760 | tf_op jit(solution)/shard_map/all_gather | solution.py:22
  37.0 329.8 %collective-permute-start = (bf16[1024,14848]{1,0:T(8,128)(2,1)}, bf16[1024,14848]{1,0:T(8,128)(2,1)}, u32[]{:S(2)}, u32[]{:S(2)}) collective-permute-start(bf16[1024,14848]{1,0:T(8,128)(2,1)} %convert_bitcast_fusion), channel_id=1, source_target_pairs={{0,4},{4,8},{8,12},{12,0},{1,5},{5,9},{9,13},{13,1},{2,6},{6,10},{... | collective-permute-start | bytes 91226120 | tf_op jit(solution)/shard_map/ppermute | solution.py:11
  366.8 329.1 %collective-permute-start.1 = (bf16[1024,14848]{1,0:T(8,128)(2,1)}, bf16[1024,14848]{1,0:T(8,128)(2,1)}, u32[]{:S(2)}, u32[]{:S(2)}) collective-permute-start(bf16[1024,14848]{1,0:T(8,128)(2,1)} %collective-permute-done), channel_id=1, source_target_pairs={{0,4},{4,8},{8,12},{12,0},{1,5},{5,9},{9,13},{13,1},{2,6},{6,10},{... | collective-permute-start | bytes 91226120 | tf_op jit(solution)/shard_map/ppermute | solution.py:11
  695.9 329.1 %collective-permute-start.2 = (bf16[1024,14848]{1,0:T(8,128)(2,1)}, bf16[1024,14848]{1,0:T(8,128)(2,1)}, u32[]{:S(2)}, u32[]{:S(2)}) collective-permute-start(bf16[1024,14848]{1,0:T(8,128)(2,1)} %collective-permute-done.1), channel_id=1, source_target_pairs={{0,4},{4,8},{8,12},{12,0},{1,5},{5,9},{9,13},{13,1},{2,6},{6,10},{... | collective-permute-start | bytes 91226120 | tf_op jit(solution)/shard_map/ppermute | solution.py:11
  758.9 286.7 %copy-start = (f32[4]{0:T(128)S(1)}, f32[4]{0:T(128)}, u32[]{:S(2)}) copy-start(f32[4]{0:T(128)} %get-tuple-element.7) | copy-start | bytes 52
  758.9 286.7 %copy-start.1 = (f32[4]{0:T(128)S(1)}, f32[4]{0:T(128)}, u32[]{:S(2)}) copy-start(f32[4]{0:T(128)} %get-tuple-element.8) | copy-start | bytes 52
  758.9 286.7 %copy-start.2 = (f32[4]{0:T(128)S(1)}, f32[4]{0:T(128)}, u32[]{:S(2)}) copy-start(f32[4]{0:T(128)} %get-tuple-element.5) | copy-start | bytes 52
  758.9 286.7 %copy-start.3 = (f32[4]{0:T(128)S(1)}, f32[4]{0:T(128)}, u32[]{:S(2)}) copy-start(f32[4]{0:T(128)} %get-tuple-element.6) | copy-start | bytes 52
  758.9 299.7 %copy-start.6 = (s32[448]{0:T(512)S(1)}, s32[448]{0:T(512)}, u32[]{:S(2)}) copy-start(s32[448]{0:T(512)} %param.9) | copy-start | bytes 5380
  759.0 305.6 %copy-start.4 = (f32[4]{0:T(128)S(1)}, f32[4]{0:T(128)}, u32[]{:S(2)}) copy-start(f32[4]{0:T(128)} %param.8) | copy-start | bytes 52
Sparse Core Ops, SparseCore 0:
  366.9 232.3 all-gather.1
where the time goes:
time: 1070 us
  waiting for transfers between devices  925 us (86%)
  matrix products  82.6 us (8%)
  other arithmetic  32.4 us (3%)
  blocking collectives  18.6 us (2%)
  between operations  13.5 us (1%)
    ppermute x3, waiting for transfers between devices, passed_along(): lax.ppermute(array, axis, [(i, (i + by) % length) for i in range(length)])  924 us
    dot_general x4, matrix products, score(): lax.dot_general(grads, piece, (((1,), (1,)), ((), ())), preferred_element...  82.4 us
    convert_element_type x1, other arithmetic, local(): slab = eigvecs[0].astype(jnp.bfloat16)  30.5 us
  transfers between devices with their start and end apart: 4, of which 3 were waited for; matrix products, arithmetic and copies ran while one was open for 6% of the time, Pallas kernels for 0%

commit v1 on v0

--- a/solution.py
+++ b/solution.py
@@ -1,9 +1,14 @@
 import jax
 import jax.numpy as jnp
 from jax import lax
+from jax.experimental import pallas as pl
+from jax.experimental.pallas import tpu as pltpu
 from jax.sharding import PartitionSpec as P
 
 SEG_MEAN = 16
+QUARTERS = 4
+PLANES = 4
+INNER, OUTER, ACROSS, SIBLING = 0, 1, 2, 3
 
 
 def passed_along(array, axis, by):
@@ -11,7 +16,7 @@
     return lax.ppermute(array, axis, [(i, (i + by) % length) for i in range(length)])
 
 
-def local(activations, out_grads, eigvecs, eigvals, segment_ids):
+def by_ring(activations, out_grads, eigvecs, eigvals, segment_ids):
     tok_rows = activations.shape[0]
     blocks = lax.axis_size("blk")
     mine = lax.axis_index("blk")
@@ -44,6 +49,330 @@
     return scores / eigvals[None, :]
 
 
+def kernel(
+    a_ref, g_ref, e_ref, out_ref, all_g,
+    slab, acts, held, stage,
+    got_g, sent_g, got_a, sent_a, local_sem, stage_sem,
+):
+    blk = lax.axis_index("blk")
+    z = lax.axis_index("rows")
+    half, core = blk // 2, blk % 2
+    upper = z >= PLANES // 2
+    toward = jnp.where(upper, -1, 1)
+    is_end = (z == 0) | (z == PLANES - 1)
+    is_mid = jnp.logical_not(is_end)
+    here = jnp.where(is_end, 0, 1)
+
+    def plane(m):
+        return jnp.where(upper, PLANES - 1 - m, m)
+
+    across = {"blk": (1 - half) * 2 + core}
+    sibling = {"blk": half * 2 + 1 - core}
+    inner = {"rows": z + toward}
+    outer = {"rows": jnp.where(is_mid, z - toward, z + toward)}
+    targets = {INNER: inner, OUTER: outer, ACROSS: across, SIBLING: sibling}
+
+    toks = a_ref.shape[0]
+    quarter = toks // QUARTERS
+    width = g_ref.shape[1]
+    depth = slab.shape[1]
+
+    def unit(h, c, m, q):
+        rows = pl.ds(pl.multiple_of(c * toks + q * quarter, 16), quarter)
+        return all_g.at[h, plane(m), rows]
+
+    def sending(channel, other, m, q, own=False):
+        h = jnp.where(other == 1, 1 - half, half)
+        dst = unit(h, core, m, q)
+        src = g_ref.at[pl.ds(pl.multiple_of(q * quarter, 16), quarter)] if own else dst
+        return pltpu.make_async_remote_copy(
+            src_ref=src,
+            dst_ref=dst,
+            send_sem=sent_g.at[channel, other, plane(m), q],
+            recv_sem=got_g.at[h, core, plane(m), q],
+            device_id=targets[channel],
+            device_id_type=pl.DeviceIdType.MESH,
+        )
+
+    def await_unit(other, c, m, q):
+        h = jnp.where(other == 1, 1 - half, half)
+        piece = unit(h, c, m, q)
+        pltpu.make_async_copy(piece, piece, got_g.at[h, c, plane(m), q]).wait()
+
+    def act_rows(h, c):
+        return acts.at[h, pl.ds(pl.multiple_of(c * toks, 16), toks)]
+
+    def act_send(index, target, h, src):
+        return pltpu.make_async_remote_copy(
+            src_ref=src,
+            dst_ref=act_rows(h, core),
+            send_sem=sent_a.at[index],
+            recv_sem=got_a.at[h, core],
+            device_id=target,
+            device_id_type=pl.DeviceIdType.MESH,
+        )
+
+    def await_acts(h, c):
+        rows = act_rows(h, c)
+        pltpu.make_async_copy(rows, rows, got_a.at[h, c]).wait()
+
+    barrier = pltpu.get_barrier_semaphore()
+    for target in (inner, across, sibling):
+        pl.semaphore_signal(barrier, inc=1, device_id=target, device_id_type=pl.DeviceIdType.MESH)
+
+    @pl.when(is_mid)
+    def _():
+        pl.semaphore_signal(barrier, inc=1, device_id=outer, device_id_type=pl.DeviceIdType.MESH)
+
+    pl.semaphore_wait(barrier, jnp.where(is_mid, 4, 3))
+
+    act_send(0, across, half, a_ref).start()
+    act_send(1, sibling, half, a_ref).start()
+
+    @pl.loop(0, QUARTERS)
+    def _(q):
+        sending(INNER, 0, here, q, own=True).start()
+
+        @pl.when(is_mid)
+        def _():
+            sending(OUTER, 0, here, q, own=True).start()
+
+        sending(ACROSS, 0, here, q, own=True).start()
+        sending(SIBLING, 0, here, q, own=True).start()
+
+    own_acts = pltpu.make_async_copy(a_ref, act_rows(half, core), local_sem.at[0])
+    own_acts.start()
+    own_grads = pltpu.make_async_copy(
+        g_ref,
+        all_g.at[half, z, pl.ds(pl.multiple_of(core * toks, 16), toks)],
+        local_sem.at[1],
+    )
+    own_grads.start()
+
+    chunk = stage.shape[1]
+    per_piece = depth // chunk
+    chunks = per_piece * PLANES
+
+    def fetch(i):
+        rows = pl.ds(pl.multiple_of((i % per_piece) * chunk, chunk), chunk)
+        cols = pl.ds(pl.multiple_of((i // per_piece) * width, 128), width)
+        return pltpu.make_async_copy(e_ref.at[0, rows, cols], stage.at[i % 2], stage_sem.at[i % 2])
+
+    fetch(0).start()
+
+    @pl.loop(0, chunks)
+    def _(i):
+        @pl.when(i + 1 < chunks)
+        def _():
+            fetch(i + 1).start()
+
+        fetch(i).wait()
+        rows = pl.ds(pl.multiple_of((i % per_piece) * chunk, chunk), chunk)
+        slab[i // per_piece, rows, :] = stage[i % 2].astype(jnp.bfloat16)
+
+    out_ref[...] = jnp.zeros_like(out_ref)
+    own_acts.wait()
+    own_grads.wait()
+    await_acts(1 - half, core)
+    act_send(2, sibling, 1 - half, act_rows(1 - half, core)).start()
+    await_acts(half, 1 - core)
+    await_acts(1 - half, 1 - core)
+
+    tile = 256
+
+    def score(other, m):
+        h = jnp.where(other == 1, 1 - half, half)
+        p = plane(m)
+        load = pltpu.make_async_copy(all_g.at[h, p], held, local_sem.at[2])
+        load.start()
+        load.wait()
+
+        @pl.loop(0, 2 * (depth // tile))
+        def _(i):
+            c, d = i % 2, i // 2
+            rows = pl.ds(pl.multiple_of(c * toks, 16), toks)
+            cols = pl.ds(pl.multiple_of(d * tile, tile), tile)
+            projected = lax.dot_general(
+                held[rows, :], slab[p, cols, :],
+                (((1,), (1,)), ((), ())), preferred_element_type=jnp.float32,
+            )
+            weighed = projected * acts[h, rows, cols].astype(jnp.float32)
+            out_ref[h, rows, :] += weighed[:, :128] + weighed[:, 128:]
+
+    @pl.loop(0, 16)
+    def _(s):
+        full = s // QUARTERS
+        q = s % QUARTERS
+
+        @pl.when(is_end)
+        def _():
+            @pl.when(s < 12)
+            def _():
+                await_unit(0, core, 1 + full, q)
+
+                @pl.when((s >= 4) | (s == 3))
+                def _():
+                    sending(ACROSS, 0, 1 + full, q).start()
+
+                sending(SIBLING, 0, 1 + full, q).start()
+
+            @pl.when((s >= 12) & (s < 15))
+            def _():
+                await_unit(1, core, 1, q)
+                sending(SIBLING, 1, 1, q).start()
+
+            @pl.when(s < 13)
+            def _():
+                late = s - 5
+                m = jnp.where(s < 4, 0, jnp.where(s == 4, 1, 2 + jnp.maximum(late, 0) // QUARTERS))
+                part = jnp.where(s < 4, q, jnp.where(s == 4, 3, jnp.maximum(late, 0) % QUARTERS))
+                await_unit(1, core, m, part)
+
+                @pl.when(s < 4)
+                def _():
+                    sending(INNER, 1, 0, q).start()
+
+                sending(SIBLING, 1, m, part).start()
+
+        @pl.when(is_mid)
+        def _():
+            @pl.when(s < 8)
+            def _():
+                await_unit(0, core, 2 + full, q)
+                sending(OUTER, 0, 2 + full, q).start()
+                sending(ACROSS, 0, 2 + full, q).start()
+                sending(SIBLING, 0, 2 + full, q).start()
+
+            @pl.when(s < 4)
+            def _():
+                await_unit(0, core, 0, q)
+                sending(INNER, 0, 0, q).start()
+                sending(SIBLING, 0, 0, q).start()
+
+            @pl.when((s >= 4) & (s < 8))
+            def _():
+                await_unit(1, core, 0, q)
+                sending(SIBLING, 1, 0, q).start()
+
+            @pl.when(s < 12)
+            def _():
+                await_unit(1, core, 1 + full, q)
+                sending(SIBLING, 1, 1 + full, q).start()
+
+            @pl.when((s >= 8) & (s < 11))
+            def _():
+                sending(OUTER, 1, 1, q).start()
+
+        end_turn = [(1, 0, 0), (4, 0, 1), (5, 1, 0), (8, 0, 2), (9, 1, 2), (12, 0, 3), (13, 1, 3), (15, 1, 1)]
+        mid_turn = [(1, 0, 1), (4, 0, 0), (5, 0, 2), (8, 1, 1), (9, 0, 3), (12, 1, 0), (13, 1, 2), (15, 1, 3)]
+        other, m, due = jnp.int32(0), jnp.int32(0), s < 0
+        for (at, end_other, end_m), (_, mid_other, mid_m) in zip(end_turn, mid_turn):
+            other = jnp.where(s == at, jnp.where(is_end, end_other, mid_other), other)
+            m = jnp.where(s == at, jnp.where(is_end, end_m, mid_m), m)
+            due = due | (s == at)
+
+        @pl.when(due)
+        def _():
+            @pl.loop(0, QUARTERS)
+            def _(part):
+                await_unit(other, 1 - core, m, part)
+
+            score(other, m)
+
+    for index in range(3):
+        act_send(index, sibling, half, a_ref).wait_send()
+
+    @pl.loop(0, PLANES * QUARTERS)
+    def _(i):
+        m, q = i // QUARTERS, i % QUARTERS
+        sending(SIBLING, 0, m, q).wait_send()
+        sending(SIBLING, 1, m, q).wait_send()
+
+        @pl.when(is_end)
+        def _():
+            @pl.when(m == 0)
+            def _():
+                sending(INNER, 0, m, q).wait_send()
+                sending(INNER, 1, m, q).wait_send()
+
+            @pl.when((m != 1) | (q == 3))
+            def _():
+                sending(ACROSS, 0, m, q).wait_send()
+
+        @pl.when(is_mid)
+        def _():
+            @pl.when(m < 2)
+            def _():
+                sending(INNER, 0, m, q).wait_send()
+
+            @pl.when(m > 0)
+            def _():
+                sending(OUTER, 0, m, q).wait_send()
+                sending(ACROSS, 0, m, q).wait_send()
+
+            @pl.when((m == 1) & (q < 3))
+            def _():
+                sending(OUTER, 1, m, q).wait_send()
+
+
+def by_kernel(activations, out_grads, eigvecs, eigvals, segment_ids):
+    toks, depth = activations.shape
+    width = out_grads.shape[1]
+    blocks = lax.axis_size("blk")
+    number = eigvals.shape[0]
+    examples = toks * blocks // SEG_MEAN
+    any_space = pl.BlockSpec(memory_space=pl.ANY)
+    token_sums, _ = pl.pallas_call(
+        kernel,
+        out_shape=(
+            jax.ShapeDtypeStruct((2, 2 * toks, 128), jnp.float32),
+            jax.ShapeDtypeStruct((2, PLANES, 2 * toks, width), jnp.bfloat16),
+        ),
+        in_specs=[any_space] * 3,
+        out_specs=(pl.BlockSpec(memory_space=pltpu.VMEM), any_space),
+        scratch_shapes=[
+            pltpu.VMEM((PLANES, depth, width), jnp.bfloat16),
+            pltpu.VMEM((2, 2 * toks, depth), jnp.bfloat16),
+            pltpu.VMEM((2 * toks, width), jnp.bfloat16),
+            pltpu.VMEM((2, min(128, depth), width), jnp.float32),
+            pltpu.SemaphoreType.DMA((2, 2, PLANES, QUARTERS)),
+            pltpu.SemaphoreType.DMA((4, 2, PLANES, QUARTERS)),
+            pltpu.SemaphoreType.DMA((2, 2)),
+            pltpu.SemaphoreType.DMA((3,)),
+            pltpu.SemaphoreType.DMA((3,)),
+            pltpu.SemaphoreType.DMA((2,)),
+        ],
+        compiler_params=pltpu.CompilerParams(
+            collective_id=0, has_side_effects=True, vmem_limit_bytes=60 * 2**20
+        ),
+        cost_estimate=pl.CostEstimate(
+            flops=2 * blocks * toks * depth * width * PLANES,
+            bytes_accessed=4 * depth * width * PLANES + 4 * blocks * toks * width * PLANES,
+            transcendentals=0,
+        ),
+    )(activations, out_grads, eigvecs)
+    token_scores = jnp.sum(token_sums.reshape(blocks * toks, 128), axis=1)
+    ids = lax.all_gather(segment_ids, "blk", tiled=True)
+    member = (ids[:, None] == jnp.arange(examples, dtype=jnp.int32)[None, :]).astype(jnp.float32)
+    scored = jnp.dot(member.T, token_scores[:, None], precision=lax.Precision.HIGHEST)
+    picked = (jnp.arange(number, dtype=jnp.int32) == lax.axis_index("blk")).astype(jnp.float32)
+    scores = lax.psum(scored * picked[None, :], ("blk", "rows"))
+    return scores / eigvals[None, :]
+
+
+def local(activations, out_grads, eigvecs, eigvals, segment_ids):
+    toks, depth = activations.shape
+    fits = (
+        lax.axis_size("blk") == 4
+        and lax.axis_size("rows") == PLANES
+        and toks % (16 * QUARTERS) == 0
+        and out_grads.shape[1] % 128 == 0
+        and depth % 256 == 0
+    )
+    run = by_kernel if fits else by_ring
+    return run(activations, out_grads, eigvecs, eigvals, segment_ids)
+
+
 def solution(mesh):
     in_specs = (
         P(("copies", "blk"), "rows"),

time: 1070 us -> 364 us (0.34)
  waiting for transfers between devices: 925 us -> 0 us
  Pallas kernels: 0 us -> 323 us
  matrix products: 82.6 us -> 0.52 us
  other arithmetic: 32.4 us -> 2.22 us
  blocking collectives: 18.6 us -> 36.5 us
  between operations: 13.5 us -> 0.72 us
    ppermute x3 -> x0, waiting for transfers between devices: 924 us -> none  [passed_along(): lax.ppermute(array, axis, [(i, (i + by) % length) for i in range(length)])]
    pallas_call x0 -> x1, Pallas kernels: none -> 323 us  [by_kernel(): pl.pallas_call(kernel, out_shape=(jax.ShapeDtypeStruct((2, 2 * toks, 128)...]
    dot_general x5 -> x1, matrix products: 82.6 us -> 0.52 us  [by_kernel(): jnp.dot(member.T, token_scores[:, None], precision=lax.Precision.HIGHEST)]
    convert_element_type x3 -> x1, other arithmetic: 31.6 us -> 0.01 us  [by_kernel(): (jnp.arange(number, dtype=jnp.int32) == lax.axis_index('blk')).astype(jnp...]
    psum x2 -> x1, blocking collectives: 18.6 us -> 31.6 us  [by_kernel(): scores = lax.psum(scored * picked[None, :], ('blk', 'rows'))]
  transfers between devices with their start and end apart: 4 -> 0, of which waited for: 3 -> 0; matrix products, arithmetic and copies ran while one was open for 6% -> 0% of each run, Pallas kernels for 0% -> 0%
where the time goes in v1:
time: 364 us
  Pallas kernels  323 us (89%)
  blocking collectives  36.5 us (10%)
    pallas_call x1, Pallas kernels, by_kernel(): pl.pallas_call(kernel, out_shape=(jax.ShapeDtypeStruct((2, 2 * toks, 128)...  323 us
    psum x1, blocking collectives, by_kernel(): scores = lax.psum(scored * picked[None, :], ('blk', 'rows'))  31.6 us

profile of v1, /device:TPU:0, one launch (start us, length us, event | category | flops | bytes accessed | tf_op | source)
XLA Modules:
  0.0 363.7 jit_solution(18005572260352830318)
XLA Ops:
  0.0 0.0 copy-start.2
  0.0 0.0 copy-start
  0.0 0.0 copy-start.1
  0.0 322.8 %shard_map.55 = (f32[2,896,128]{2,1,0:T(8,128)}, bf16[2,4,896,3712]{3,2,1,0:T(8,128)(2,1)}) custom-call(bf16[448,1024]{1,0:T(8,128)(2,1)} %a_ref.1, bf16[448,3712]{1,0:T(8,128)(2,1)} %g_ref.1, f32[1,1024,14848]{2,1,0:T(8,128)} %e_ref.1), custom_call_target="tpu_custom_call" | custom-call | flops 54492397568 | bytes 167247872 | tf_op jit(solution)/shard_map/pallas_call | solution.py:325
  322.8 1.5 reduce_sum.9
  324.4 0.0 copy-done.2
  324.4 0.6 dynamic-slice
  325.6 0.0 copy-done
  325.6 0.3 dynamic-update-slice
  325.9 4.9 %all-reduce = s32[1792]{0:T(1024)S(1)} all-reduce(s32[1792]{0:T(1024)S(1)} %dynamic-update-slice), channel_id=1, replica_groups=mesh['copies'=2,'blk'=4,'rows'=4] {'blk'}, use_global_device_ids=true, to_apply=%add | all-reduce | flops 1792 | bytes 14336
  330.9 0.5 convolution_bitcast_fusion
  331.4 0.1 broadcast_multiply_fusion
  331.5 31.6 %psum.7 = f32[112,4]{0,1:T(4,128)S(1)} all-reduce(f32[112,4]{0,1:T(4,128)S(1)} %broadcast_multiply_fusion), channel_id=1, replica_groups=mesh['copies'=2,'blk'=4,'rows'=4] {'blk','rows'}, use_global_device_ids=true, to_apply=%region_1.0 | all-reduce | flops 448 | bytes 3584 | tf_op jit(solution)/shard_map/psum | solution.py:359
  363.0 0.0 copy-done.1
  363.0 0.7 broadcast_divide_fusion
  (3 shorter events, 0.0 us)
Async XLA Ops:
  0.0 324.4 %copy-start.2 = (u32[32]{0:T(128)S(1)}, u32[32]{0:T(128)}, u32[]{:S(2)}) copy-start(u32[32]{0:T(128)} %constant.10) | copy-start | bytes 388
  0.0 325.6 %copy-start = (s32[448]{0:T(512)S(1)}, s32[448]{0:T(512)}, u32[]{:S(2)}) copy-start(s32[448]{0:T(512)} %param.9) | copy-start | bytes 5380
  0.0 363.0 %copy-start.1 = (f32[4]{0:T(128)S(1)}, f32[4]{0:T(128)}, u32[]{:S(2)}) copy-start(f32[4]{0:T(128)} %param.8) | copy-start | bytes 52

commit v2 on v1

v2 whole, which is shorter than its diff:
```python
import jax
import jax.numpy as jnp
from jax import lax
from jax.experimental import pallas as pl
from jax.experimental.pallas import tpu as pltpu
from jax.sharding import PartitionSpec as P

SEG_MEAN = 16
QUARTERS = 4
PLANES = 4
INNER, OUTER, ACROSS, SIBLING = 0, 1, 2, 3


def passed_along(array, axis, by):
    length = lax.axis_size(axis)
    return lax.ppermute(array, axis, [(i, (i + by) % length) for i in range(length)])


def by_ring(activations, out_grads, eigvecs, eigvals, segment_ids):
    tok_rows = activations.shape[0]
    blocks = lax.axis_size("blk")
    mine = lax.axis_index("blk")
    number = eigvals.shape[0]
    examples = tok_rows * blocks // SEG_MEAN
    widened = activations.astype(jnp.float32)
    slab = eigvecs[0].astype(jnp.bfloat16)
    grads = lax.all_gather(out_grads, "rows", axis=1, tiled=True)
    columns = jnp.arange(number, dtype=jnp.int32)

    def score(piece, owner, totals):
        projected = lax.dot_general(
            grads, piece, (((1,), (1,)), ((), ())), preferred_element_type=jnp.float32
        )
        partial_sum = jnp.sum(projected * widened, axis=1)
        picked = (columns == owner).astype(jnp.float32)
        return totals + partial_sum[:, None] * picked[None, :]

    totals = score(slab, mine, jnp.zeros((tok_rows, number), jnp.float32))
    moving = slab
    for step in range(blocks - 1):
        moving = passed_along(moving, "blk", 1)
        totals = score(moving, (mine - step - 1) % blocks, totals)
    member = (segment_ids[:, None] == jnp.arange(examples, dtype=jnp.int32)[None, :]).astype(
        jnp.float32
    )
    full_tokens = lax.psum(totals, "rows")
    local_scores = jnp.dot(member.T, full_tokens, precision=lax.Precision.HIGHEST)
    scores = lax.psum(local_scores, "blk")
    return scores / eigvals[None, :]


def turns(s_list):
    return {2 * s + i: job for s, jobs in s_list.items() for i, job in enumerate(jobs)}


END_TURNS = turns({
    0: [(0, 0, 0, 0), (0, 0, 1, 0)],
    2: [(0, 1, 0, 0)],
    3: [(1, 0, 0, 0)],
    4: [(0, 1, 1, 0), (1, 0, 1, 0)],
    6: [(0, 2, 0, 0)],
    7: [(1, 2, 0, 0)],
    8: [(0, 2, 1, 0)],
    9: [(1, 2, 1, 0), (1, 1, 0, 0)],
    10: [(1, 1, 1, 0)],
})
MID_TURNS = turns({
    0: [(0, 1, 0, 0), (0, 1, 1, 0)],
    2: [(0, 0, 0, 0)],
    3: [(0, 2, 0, 0)],
    4: [(0, 0, 1, 0), (0, 2, 1, 0)],
    5: [(1, 1, 0, 0)],
    6: [(1, 1, 1, 0), (0, 3, 0, 0)],
    7: [(1, 0, 0, 0)],
    8: [(0, 3, 1, 0)],
    9: [(1, 3, 0, 0)],
    10: [(1, 2, 0, 0), (1, 3, 1, 0)],
    11: [(0, 3, 0, 1), (0, 3, 1, 1)],
    12: [(1, 3, 0, 1), (1, 3, 1, 1)],
    13: [(1, 2, 1, 0), (1, 0, 1, 0)],
})
STEPS = 14


def kernel(
    a_ref, g_ref, e_ref, i_ref, out_ref, all_g,
    slab, acts, held, stage, sums, ids, by_plane, by_block,
    got_g, sent_g, got_a, sent_a, got_v, sent_v, got_i, sent_i, got_s, sent_s, local_sem, stage_sem,
):
    mesh_id = pl.DeviceIdType.MESH
    blk = lax.axis_index("blk")
    z = lax.axis_index("rows")
    y = lax.axis_index("copies")
    half, core = blk // 2, blk % 2
    upper = z >= PLANES // 2
    toward = jnp.where(upper, -1, 1)
    is_end = (z == 0) | (z == PLANES - 1)
    is_mid = jnp.logical_not(is_end)
    here = jnp.where(is_end, 0, 1)

    def plane(m):
        return jnp.where(upper, PLANES - 1 - m, m)

    across = {"blk": (1 - half) * 2 + core}
    sibling = {"blk": half * 2 + 1 - core}
    inner = {"rows": z + toward}
    outer = {"rows": jnp.where(is_mid, z - toward, z + toward)}
    beside = {"copies": 1 - y}
    targets = {INNER: inner, OUTER: outer, ACROSS: across, SIBLING: sibling}

    toks = a_ref.shape[0]
    quarter = toks // QUARTERS
    width = g_ref.shape[1]
    depth = slab.shape[1]

    def unit(h, c, m, q):
        rows = pl.ds(pl.multiple_of(c * toks + q * quarter, 16), quarter)
        return all_g.at[h, plane(m), rows]

    def column(other):
        return jnp.where(other == 1, 1 - half, half)

    def sending(channel, other, m, q, own=False):
        h = column(other)
        dst = unit(h, core, m, q)
        src = g_ref.at[pl.ds(pl.multiple_of(q * quarter, 16), quarter)] if own else dst
        return pltpu.make_async_remote_copy(
            src_ref=src,
            dst_ref=dst,
            send_sem=sent_g.at[channel, other, plane(m), q],
            recv_sem=got_g.at[h, core, plane(m), q],
            device_id=targets[channel],
            device_id_type=mesh_id,
        )

    def await_unit(other, c, m, q):
        h = column(other)
        piece = unit(h, c, m, q)
        pltpu.make_async_copy(piece, piece, got_g.at[h, c, plane(m), q]).wait()

    def act_rows(h, c):
        return acts.at[h, pl.ds(pl.multiple_of(c * toks, 16), toks)]

    def act_send(index, target, h, src):
        return pltpu.make_async_remote_copy(
            src_ref=src,
            dst_ref=act_rows(h, core),
            send_sem=sent_a.at[index],
            recv_sem=got_a.at[h, core],
            device_id=target,
            device_id_type=mesh_id,
        )

    def await_acts(h, c):
        rows = act_rows(h, c)
        pltpu.make_async_copy(rows, rows, got_a.at[h, c]).wait()

    strip = depth // 2 // QUARTERS

    def strip_rows(which, u):
        return pl.ds(pl.multiple_of(which * (depth // 2) + u * strip, 16), strip)

    def slab_send(target, source, u):
        return pltpu.make_async_remote_copy(
            src_ref=slab.at[source, strip_rows(y, u)],
            dst_ref=slab.at[PLANES, strip_rows(y, u)],
            send_sem=sent_v.at[u],
            recv_sem=got_v.at[y, u],
            device_id=target,
            device_id_type=mesh_id,
        )

    def await_slab(which, u):
        rows = slab.at[PLANES, strip_rows(which, u)]
        pltpu.make_async_copy(rows, rows, got_v.at[which, u]).wait()

    def ids_send(j):
        return pltpu.make_async_remote_copy(
            src_ref=i_ref,
            dst_ref=ids.at[blk],
            send_sem=sent_i.at[j - 1],
            recv_sem=got_i.at[blk],
            device_id={"blk": (blk + j) % 4},
            device_id_type=mesh_id,
        )

    barrier = pltpu.get_barrier_semaphore()
    for j in range(1, 4):
        for target in ({"blk": (blk + j) % 4}, {"rows": (z + j) % PLANES}):
            pl.semaphore_signal(barrier, inc=1, device_id=target, device_id_type=mesh_id)
    pl.semaphore_signal(barrier, inc=1, device_id=beside, device_id_type=mesh_id)
    pl.semaphore_wait(barrier, 7)

    act_send(0, across, half, a_ref).start()
    act_send(1, sibling, half, a_ref).start()

    @pl.loop(0, QUARTERS)
    def _(q):
        sending(INNER, 0, here, q, own=True).start()

        @pl.when(is_mid)
        def _():
            sending(OUTER, 0, here, q, own=True).start()

        sending(ACROSS, 0, here, q, own=True).start()
        sending(SIBLING, 0, here, q, own=True).start()

    for j in range(1, 4):
        ids_send(j).start()

    @pl.when(is_end)
    def _():
        act_send(3, inner, 2 + half, a_ref).start()

    own_acts = pltpu.make_async_copy(a_ref, act_rows(half, core), local_sem.at[0])
    own_acts.start()
    own_grads = pltpu.make_async_copy(
        g_ref,
        all_g.at[half, z, pl.ds(pl.multiple_of(core * toks, 16), toks)],
        local_sem.at[1],
    )
    own_grads.start()

    chunk = stage.shape[1]
    per_piece = depth // chunk
    chunks = per_piece * PLANES

    def fetch_piece(i):
        return plane((PLANES - 1 + i // per_piece) % PLANES)

    def fetch(i):
        rows = pl.ds(pl.multiple_of((i % per_piece) * chunk, chunk), chunk)
        cols = pl.ds(pl.multiple_of(fetch_piece(i) * width, 128), width)
        return pltpu.make_async_copy(e_ref.at[0, rows, cols], stage.at[i % 2], stage_sem.at[i % 2])

    fetch(0).start()

    @pl.loop(0, chunks)
    def _(i):
        @pl.when(i + 1 < chunks)
        def _():
            fetch(i + 1).start()

        fetch(i).wait()
        rows = pl.ds(pl.multiple_of((i % per_piece) * chunk, chunk), chunk)
        slab[fetch_piece(i), rows, :] = stage[i % 2].astype(jnp.bfloat16)

        @pl.when((i == per_piece - 1) & is_end)
        def _():
            @pl.loop(0, QUARTERS)
            def _(u):
                slab_send(inner, plane(PLANES - 1), u).start()

    sums[...] = jnp.zeros_like(sums)
    ids[blk] = i_ref[...]
    own_acts.wait()
    own_grads.wait()
    await_acts(1 - half, core)
    act_send(2, sibling, 1 - half, act_rows(1 - half, core)).start()

    @pl.when(is_end)
    def _():
        act_send(4, inner, 2 + 1 - half, act_rows(1 - half, core)).start()

    await_acts(half, 1 - core)
    await_acts(1 - half, 1 - core)

    tile = 256
    part = toks // 2

    def score(other, m, second, for_end):
        h = column(other)
        p = plane(m)
        for c in range(2):
            pltpu.make_async_copy(
                all_g.at[h, p, pl.ds(pl.multiple_of(c * toks + second * part, 16), part)],
                held.at[pl.ds(c * part, part)],
                local_sem.at[2 + c],
            ).start()
        for c in range(2):
            pltpu.make_async_copy(
                all_g.at[h, p, pl.ds(pl.multiple_of(c * toks + second * part, 16), part)],
                held.at[pl.ds(c * part, part)],
                local_sem.at[2 + c],
            ).wait()
        which = jnp.where(for_end == 1, PLANES, p)

        @pl.loop(0, depth // tile)
        def _(d):
            cols = pl.ds(pl.multiple_of(d * tile, tile), tile)
            projected = lax.dot_general(
                held[...], slab[which, cols, :],
                (((1,), (1,)), ((), ())), preferred_element_type=jnp.float32,
            )
            for c in range(2):
                rows = pl.ds(pl.multiple_of(c * toks + second * part, 16), part)
                factor = acts[h + 2 * for_end, rows, cols].astype(jnp.float32)
                weighed = projected[c * part:(c + 1) * part] * factor
                sums[h, rows, :] += weighed[:, :128] + weighed[:, 128:]

    @pl.loop(0, STEPS)
    def _(s):
        full = s // QUARTERS
        q = s % QUARTERS

        @pl.when(is_end)
        def _():
            @pl.when(s < 8)
            def _():
                await_unit(0, core, 1 + full, q)

                @pl.when(s >= 3)
                def _():
                    sending(ACROSS, 0, 1 + full, q).start()

                sending(SIBLING, 0, 1 + full, q).start()

            @pl.when((s >= 8) & (s < 11))
            def _():
                await_unit(1, core, 1, q)
                sending(SIBLING, 1, 1, q).start()

            @pl.when(s < 9)
            def _():
                late = jnp.maximum(s - 5, 0)
                m = jnp.where(s < 4, 0, jnp.where(s == 4, 1, 2))
                r = jnp.where(s < 4, q, jnp.where(s == 4, 3, late))
                await_unit(1, core, m, r)

                @pl.when(s == 3)
                def _():
                    sending(INNER, 1, 0, 3).start()

                sending(SIBLING, 1, m, r).start()

        @pl.when(is_mid)
        def _():
            @pl.when(s < 8)
            def _():
                await_unit(0, core, 2 + full, q)

                @pl.when(s < 4)
                def _():
                    sending(OUTER, 0, 2, q).start()

                @pl.when(s >= 4)
                def _():
                    sending(ACROSS, 0, 3, q).start()

                sending(SIBLING, 0, 2 + full, q).start()

            @pl.when((s >= 8) & (s < 12))
            def _():
                await_unit(1, core, 2, q)
                sending(SIBLING, 1, 2, q).start()

            @pl.when(s < 4)
            def _():
                await_unit(0, core, 0, q)
                sending(INNER, 0, 0, q).start()

                @pl.when(s < 3)
                def _():
                    sending(ACROSS, 0, 0, q).start()

                sending(SIBLING, 0, 0, q).start()

            @pl.when(s < 11)
            def _():
                m = jnp.where(s < 4, 1, jnp.where(s < 7, 0, 3))
                r = jnp.where(s < 7, q, jnp.maximum(s - 7, 0))
                await_unit(1, core, m, r)
                sending(SIBLING, 1, m, r).start()

            @pl.when((s >= 4) & (s < 8))
            def _():
                sending(INNER, 1, 1, q).start()

                @pl.when(s < 7)
                def _():
                    sending(OUTER, 1, 1, q).start()

            @pl.when((s >= 7) & (s < 11))
            def _():
                await_slab(y, s - 7)
                slab_send(beside, PLANES, s - 7).start()

            @pl.when(s == 11)
            def _():
                await_acts(2 + half, core)
                act_send(3, sibling, 2 + half, act_rows(2 + half, core)).start()
                await_acts(2 + 1 - half, core)
                act_send(4, sibling, 2 + 1 - half, act_rows(2 + 1 - half, core)).start()

                @pl.loop(0, QUARTERS)
                def _(u):
                    await_slab(1 - y, u)

                await_acts(2 + half, 1 - core)
                await_acts(2 + 1 - half, 1 - core)

            @pl.when(s == 12)
            def _():
                await_unit(1, core, 0, 3)
                sending(SIBLING, 1, 0, 3).start()

        @pl.loop(0, 2)
        def _(i):
            turn = 2 * s + i
            job = [jnp.int32(0)] * 4
            due = turn < 0
            for at in sorted(set(END_TURNS) | set(MID_TURNS)):
                for table, mine in ((END_TURNS, is_end), (MID_TURNS, is_mid)):
                    if at in table:
                        now = (turn == at) & mine
                        job = [jnp.where(now, new, old) for new, old in zip(table[at], job)]
                        due = due | now
            other, m, second, for_end = job

            @pl.when(due)
            def _():
                @pl.when(for_end == 0)
                def _():
                    await_unit(other, 1 - core, m, 2 * second)
                    await_unit(other, 1 - core, m, 2 * second + 1)

                score(other, m, second, for_end)

    for j in range(1, 4):
        taken = (blk + j) % 4
        pltpu.make_async_copy(ids.at[taken], ids.at[taken], got_i.at[taken]).wait()
    spots = out_ref.shape[1]
    example = lax.broadcasted_iota(jnp.int32, (spots, toks), 0)
    total = jnp.zeros((spots, 128), jnp.float32)
    for b in range(4):
        member = (ids[b, 0:1, :] == example).astype(jnp.float32)
        total += jnp.dot(
            member, sums[b // 2, (b % 2) * toks:(b % 2 + 1) * toks, :],
            precision=lax.Precision.HIGHEST, preferred_element_type=jnp.float32,
        )
    across_lanes = lax.dot_general(
        jnp.ones((8, 128), jnp.float32), total, (((1,), (1,)), ((), ())),
        precision=lax.Precision.HIGHEST, preferred_element_type=jnp.float32,
    )
    mine = lax.broadcasted_iota(jnp.int32, (8, spots), 0) == blk
    by_plane[z] = jnp.where(mine, across_lanes, 0.0)

    def shared(buffer, axis, me, phase):
        def sent(j):
            return pltpu.make_async_remote_copy(
                src_ref=buffer.at[me],
                dst_ref=buffer.at[me],
                send_sem=sent_s.at[phase, j - 1],
                recv_sem=got_s.at[phase, me],
                device_id={axis: (me + j) % 4},
                device_id_type=mesh_id,
            )

        for j in range(1, 4):
            sent(j).start()
        for j in range(1, 4):
            slot = (me + j) % 4
            pltpu.make_async_copy(buffer.at[slot], buffer.at[slot], got_s.at[phase, slot]).wait()
        result = (buffer[0] + buffer[1]) + (buffer[2] + buffer[3])
        for j in range(1, 4):
            sent(j).wait_send()
        return result

    by_block[blk] = shared(by_plane, "rows", z, 0)
    out_ref[...] = shared(by_block, "blk", blk, 1)

    for j in range(1, 4):
        ids_send(j).wait_send()
    for index in range(5):
        act_send(index, sibling, half, a_ref).wait_send()

    @pl.loop(0, QUARTERS)
    def _(u):
        slab_send(beside, PLANES, u).wait_send()

    @pl.loop(0, PLANES * QUARTERS)
    def _(i):
        m, q = i // QUARTERS, i % QUARTERS

        @pl.when(is_mid | (m < 3))
        def _():
            sending(SIBLING, 0, m, q).wait_send()
            sending(SIBLING, 1, m, q).wait_send()

        @pl.when(is_end)
        def _():
            @pl.when(m == 0)
            def _():
                sending(INNER, 0, m, q).wait_send()

                @pl.when(q == 3)
                def _():
                    sending(INNER, 1, m, q).wait_send()

            @pl.when((m == 0) | (m == 2) | ((m == 1) & (q == 3)))
            def _():
                sending(ACROSS, 0, m, q).wait_send()

        @pl.when(is_mid)
        def _():
            @pl.when(m < 2)
            def _():
                sending(INNER, 0, m, q).wait_send()

            @pl.when((m == 1) | (m == 2))
            def _():
                sending(OUTER, 0, m, q).wait_send()

            @pl.when(m == 1)
            def _():
                sending(INNER, 1, m, q).wait_send()

                @pl.when(q < 3)
                def _():
                    sending(OUTER, 1, m, q).wait_send()

            @pl.when((m == 1) | (m == 3) | ((m == 0) & (q < 3)))
            def _():
                sending(ACROSS, 0, m, q).wait_send()


def by_kernel(activations, out_grads, eigvecs, eigvals, segment_ids):
    toks, depth = activations.shape
    width = out_grads.shape[1]
    blocks = lax.axis_size("blk")
    number = eigvals.shape[0]
    examples = toks * blocks // SEG_MEAN
    spots = -(-examples // 128) * 128
    any_space = pl.BlockSpec(memory_space=pl.ANY)
    in_vmem = pl.BlockSpec(memory_space=pltpu.VMEM)
    scores, _ = pl.pallas_call(
        kernel,
        out_shape=(
            jax.ShapeDtypeStruct((8, spots), jnp.float32),
            jax.ShapeDtypeStruct((2, PLANES, 2 * toks, width), jnp.bfloat16),
        ),
        in_specs=[any_space] * 3 + [in_vmem],
        out_specs=(in_vmem, any_space),
        scratch_shapes=[
            pltpu.VMEM((PLANES + 1, depth, width), jnp.bfloat16),
            pltpu.VMEM((4, 2 * toks, depth), jnp.bfloat16),
            pltpu.VMEM((toks, width), jnp.bfloat16),
            pltpu.VMEM((2, 64, width), jnp.float32),
            pltpu.VMEM((2, 2 * toks, 128), jnp.float32),
            pltpu.VMEM((4, 8, toks), jnp.int32),
            pltpu.VMEM((4, 8, spots), jnp.float32),
            pltpu.VMEM((4, 8, spots), jnp.float32),
            pltpu.SemaphoreType.DMA((2, 2, PLANES, QUARTERS)),
            pltpu.SemaphoreType.DMA((4, 2, PLANES, QUARTERS)),
            pltpu.SemaphoreType.DMA((4, 2)),
            pltpu.SemaphoreType.DMA((5,)),
            pltpu.SemaphoreType.DMA((2, QUARTERS)),
            pltpu.SemaphoreType.DMA((QUARTERS,)),
            pltpu.SemaphoreType.DMA((4,)),
            pltpu.SemaphoreType.DMA((3,)),
            pltpu.SemaphoreType.DMA((2, 4)),
            pltpu.SemaphoreType.DMA((2, 3)),
            pltpu.SemaphoreType.DMA((4,)),
            pltpu.SemaphoreType.DMA((2,)),
        ],
        compiler_params=pltpu.CompilerParams(
            collective_id=0, has_side_effects=True, vmem_limit_bytes=60 * 2**20
        ),
        cost_estimate=pl.CostEstimate(
            flops=2 * blocks * toks * depth * width * PLANES,
            bytes_accessed=4 * depth * width * PLANES + 4 * blocks * toks * width * PLANES,
            transcendentals=0,
        ),
    )(activations, out_grads, eigvecs, jnp.broadcast_to(segment_ids[None, :], (8, toks)))
    return scores[:number, :examples].T / eigvals[None, :]


def local(activations, out_grads, eigvecs, eigvals, segment_ids):
    toks, depth = activations.shape
    fits = (
        lax.axis_size("blk") == 4
        and lax.axis_size("copies") == 2
        and eigvals.shape[0] == 4
        and lax.axis_size("rows") == PLANES
        and toks % (16 * QUARTERS) == 0
        and out_grads.shape[1] % 128 == 0
        and depth % 256 == 0
    )
    run = by_kernel if fits else by_ring
    return run(activations, out_grads, eigvecs, eigvals, segment_ids)


def solution(mesh):
    in_specs = (
        P(("copies", "blk"), "rows"),
        P(("copies", "blk"), "rows"),
        P("blk", "rows", None),
        P(),
        P(("copies", "blk")),
    )
    out_specs = P("copies", None)
    return jax.shard_map(local, mesh=mesh, in_specs=in_specs, out_specs=out_specs, check_vma=False)
```

time: 364 us -> 321 us (0.88)
  blocking collectives: 36.5 us -> 0 us
  Pallas kernels: 323 us -> 317 us
    psum x1 -> x0, blocking collectives: 31.6 us -> none  [by_kernel(): scores = lax.psum(scored * picked[None, :], ('blk', 'rows'))]
    pallas_call x1, Pallas kernels: 323 us -> 317 us  [by_kernel(): pl.pallas_call(kernel, out_shape=(jax.ShapeDtypeStruct((8, spots), jnp.fl...]
    unnamed x1 -> x0, blocking collectives: 4.95 us -> none
where the time goes in v2:
time: 321 us; the launch traced here: 319 us
  Pallas kernels  317 us (99%)
    pallas_call x1, Pallas kernels, by_kernel(): pl.pallas_call(kernel, out_shape=(jax.ShapeDtypeStruct((8, spots), jnp.fl...  317 us

profile of v2, /device:TPU:0, one launch (start us, length us, event | category | flops | bytes accessed | tf_op | source)
XLA Modules:
  0.0 319.4 jit_solution(14972931108407506735)
XLA Ops:
  0.0 1.3 broadcast_in_dim.2.i_ref
  1.3 0.0 copy-start
  1.3 316.7 %shard_map.55 = (f32[8,128]{1,0:T(8,128)}, bf16[2,4,896,3712]{3,2,1,0:T(8,128)(2,1)}) custom-call(bf16[448,1024]{1,0:T(8,128)(2,1)} %a_ref.1, bf16[448,3712]{1,0:T(8,128)(2,1)} %g_ref.1, f32[1,1024,14848]{2,1,0:T(8,128)} %e_ref.1, s32[8,448]{1,0:T(8,128)} %broadcast_in_dim.2.i_ref), custom_call_target="tpu_custom_call" | custom-call | flops 54492397568 | bytes 167247872 | tf_op jit(solution)/shard_map/pallas_call | solution.py:536
  318.0 0.0 copy-done
  318.0 1.3 divide_bitcast_fusion
Async XLA Ops:
  1.3 316.7 %copy-start = (f32[4]{0:T(128)S(1)}, f32[4]{0:T(128)}, u32[]{:S(2)}) copy-start(f32[4]{0:T(128)} %param.8) | copy-start | bytes 52

commit v3 on v2

--- a/solution.py
+++ b/solution.py
@@ -49,8 +49,11 @@
     return scores / eigvals[None, :]
 
 
+AT_ONCE = 4
+
+
 def turns(s_list):
-    return {2 * s + i: job for s, jobs in s_list.items() for i, job in enumerate(jobs)}
+    return {AT_ONCE * s + i: job for s, jobs in s_list.items() for i, job in enumerate(jobs)}
 
 
 END_TURNS = turns({
@@ -68,18 +71,16 @@
     0: [(0, 1, 0, 0), (0, 1, 1, 0)],
     2: [(0, 0, 0, 0)],
     3: [(0, 2, 0, 0)],
-    4: [(0, 0, 1, 0), (0, 2, 1, 0)],
-    5: [(1, 1, 0, 0)],
-    6: [(1, 1, 1, 0), (0, 3, 0, 0)],
-    7: [(1, 0, 0, 0)],
+    4: [(1, 1, 0, 0), (0, 0, 1, 0)],
+    5: [(0, 2, 1, 0)],
+    6: [(1, 1, 1, 0)],
+    7: [(0, 3, 0, 0), (1, 3, 0, 0)],
     8: [(0, 3, 1, 0)],
-    9: [(1, 3, 0, 0)],
-    10: [(1, 2, 0, 0), (1, 3, 1, 0)],
-    11: [(0, 3, 0, 1), (0, 3, 1, 1)],
-    12: [(1, 3, 0, 1), (1, 3, 1, 1)],
-    13: [(1, 2, 1, 0), (1, 0, 1, 0)],
+    9: [(1, 3, 1, 0), (1, 2, 0, 0)],
+    10: [(0, 3, 0, 1), (0, 3, 1, 1), (1, 3, 0, 1), (1, 3, 1, 1)],
+    11: [(1, 0, 0, 0), (1, 0, 1, 0), (1, 2, 1, 0)],
 })
-STEPS = 14
+STEPS = 12
 
 
 def kernel(
@@ -268,28 +269,40 @@
     tile = 256
     part = toks // 2
 
-    def score(other, m, second, for_end):
+    def loads(job, slot):
+        other, m, second, _ = job
+        return [
+            pltpu.make_async_copy(
+                all_g.at[column(other), plane(m), pl.ds(pl.multiple_of(c * toks + second * part, 16), part)],
+                held.at[slot, pl.ds(c * part, part)],
+                local_sem.at[2 + 2 * slot + c],
+            )
+            for c in range(2)
+        ]
+
+    def begin(job, slot):
+        other, m, second, for_end = job
+
+        @pl.when(for_end == 0)
+        def _():
+            await_unit(other, 1 - core, m, 2 * second)
+            await_unit(other, 1 - core, m, 2 * second + 1)
+
+        for load in loads(job, slot):
+            load.start()
+
+    def score(job, slot):
+        other, m, second, for_end = job
         h = column(other)
-        p = plane(m)
-        for c in range(2):
-            pltpu.make_async_copy(
-                all_g.at[h, p, pl.ds(pl.multiple_of(c * toks + second * part, 16), part)],
-                held.at[pl.ds(c * part, part)],
-                local_sem.at[2 + c],
-            ).start()
-        for c in range(2):
-            pltpu.make_async_copy(
-                all_g.at[h, p, pl.ds(pl.multiple_of(c * toks + second * part, 16), part)],
-                held.at[pl.ds(c * part, part)],
-                local_sem.at[2 + c],
-            ).wait()
-        which = jnp.where(for_end == 1, PLANES, p)
+        for load in loads(job, slot):
+            load.wait()
+        which = jnp.where(for_end == 1, PLANES, plane(m))
 
         @pl.loop(0, depth // tile)
         def _(d):
             cols = pl.ds(pl.multiple_of(d * tile, tile), tile)
             projected = lax.dot_general(
-                held[...], slab[which, cols, :],
+                held[slot], slab[which, cols, :],
                 (((1,), (1,)), ((), ())), preferred_element_type=jnp.float32,
             )
             for c in range(2):
@@ -298,6 +311,24 @@
                 weighed = projected[c * part:(c + 1) * part] * factor
                 sums[h, rows, :] += weighed[:, :128] + weighed[:, 128:]
 
+    def job_at(turn):
+        job = [jnp.int32(0)] * 4
+        for at in sorted(set(END_TURNS) | set(MID_TURNS)):
+            for table, mine in ((END_TURNS, is_end), (MID_TURNS, is_mid)):
+                if at in table:
+                    now = (turn == at) & mine
+                    job = [jnp.where(now, new, old) for new, old in zip(table[at], job)]
+        return job
+
+    def jobs_in(step):
+        count = jnp.int32(0)
+        for at in range(STEPS):
+            counts = [
+                sum(at * AT_ONCE + i in table for i in range(AT_ONCE)) for table in (END_TURNS, MID_TURNS)
+            ]
+            count = jnp.where(step == at, jnp.where(is_end, counts[0], counts[1]), count)
+        return count
+
     @pl.loop(0, STEPS)
     def _(s):
         full = s // QUARTERS
@@ -359,19 +390,25 @@
                 await_unit(0, core, 0, q)
                 sending(INNER, 0, 0, q).start()
 
-                @pl.when(s < 3)
-                def _():
-                    sending(ACROSS, 0, 0, q).start()
+                @pl.when(s == 0)
+                def _():
+                    sending(ACROSS, 0, 0, 0).start()
 
                 sending(SIBLING, 0, 0, q).start()
 
-            @pl.when(s < 11)
-            def _():
-                m = jnp.where(s < 4, 1, jnp.where(s < 7, 0, 3))
-                r = jnp.where(s < 7, q, jnp.maximum(s - 7, 0))
+            @pl.when((s >= 1) & (s < 12))
+            def _():
+                turn = jnp.maximum(s - 1, 0)
+                m = jnp.where(turn < 4, 1, jnp.where((turn == 4) | (turn > 8), 0, 3))
+                r = jnp.where(turn < 5, turn % QUARTERS, (turn - 5 + 5 * QUARTERS) % QUARTERS)
+                r = jnp.where(turn > 8, turn - 8, r)
                 await_unit(1, core, m, r)
                 sending(SIBLING, 1, m, r).start()
 
+            @pl.when((s >= 8) & (s < 10))
+            def _():
+                sending(ACROSS, 0, 0, jnp.maximum(s - 7, 0)).start()
+
             @pl.when((s >= 4) & (s < 8))
             def _():
                 sending(INNER, 1, 1, q).start()
@@ -380,12 +417,13 @@
                 def _():
                     sending(OUTER, 1, 1, q).start()
 
-            @pl.when((s >= 7) & (s < 11))
-            def _():
-                await_slab(y, s - 7)
-                slab_send(beside, PLANES, s - 7).start()
-
-            @pl.when(s == 11)
+            @pl.when((s >= 6) & (s < 10))
+            def _():
+                u = jnp.maximum(s - 6, 0)
+                await_slab(y, u)
+                slab_send(beside, PLANES, u).start()
+
+            @pl.when(s == 10)
             def _():
                 await_acts(2 + half, core)
                 act_send(3, sibling, 2 + half, act_rows(2 + half, core)).start()
@@ -399,32 +437,26 @@
                 await_acts(2 + half, 1 - core)
                 await_acts(2 + 1 - half, 1 - core)
 
-            @pl.when(s == 12)
+            @pl.when(s == 11)
             def _():
                 await_unit(1, core, 0, 3)
                 sending(SIBLING, 1, 0, 3).start()
 
-        @pl.loop(0, 2)
+        count = jobs_in(s)
+
+        @pl.when(count > 0)
+        def _():
+            begin(job_at(AT_ONCE * s), 0)
+
+        @pl.loop(0, AT_ONCE)
         def _(i):
-            turn = 2 * s + i
-            job = [jnp.int32(0)] * 4
-            due = turn < 0
-            for at in sorted(set(END_TURNS) | set(MID_TURNS)):
-                for table, mine in ((END_TURNS, is_end), (MID_TURNS, is_mid)):
-                    if at in table:
-                        now = (turn == at) & mine
-                        job = [jnp.where(now, new, old) for new, old in zip(table[at], job)]
-                        due = due | now
-            other, m, second, for_end = job
-
-            @pl.when(due)
-            def _():
-                @pl.when(for_end == 0)
-                def _():
-                    await_unit(other, 1 - core, m, 2 * second)
-                    await_unit(other, 1 - core, m, 2 * second + 1)
-
-                score(other, m, second, for_end)
+            @pl.when(i + 1 < count)
+            def _():
+                begin(job_at(AT_ONCE * s + i + 1), (i + 1) % 2)
+
+            @pl.when(i < count)
+            def _():
+                score(job_at(AT_ONCE * s + i), i % 2)
 
     for j in range(1, 4):
         taken = (blk + j) % 4
@@ -544,7 +576,7 @@
         scratch_shapes=[
             pltpu.VMEM((PLANES + 1, depth, width), jnp.bfloat16),
             pltpu.VMEM((4, 2 * toks, depth), jnp.bfloat16),
-            pltpu.VMEM((toks, width), jnp.bfloat16),
+            pltpu.VMEM((2, toks, width), jnp.bfloat16),
             pltpu.VMEM((2, 64, width), jnp.float32),
             pltpu.VMEM((2, 2 * toks, 128), jnp.float32),
             pltpu.VMEM((4, 8, toks), jnp.int32),
@@ -560,7 +592,7 @@
             pltpu.SemaphoreType.DMA((3,)),
             pltpu.SemaphoreType.DMA((2, 4)),
             pltpu.SemaphoreType.DMA((2, 3)),
-            pltpu.SemaphoreType.DMA((4,)),
+            pltpu.SemaphoreType.DMA((6,)),
             pltpu.SemaphoreType.DMA((2,)),
         ],
         compiler_params=pltpu.CompilerParams(

time: 321 us -> 302 us (0.941)
  Pallas kernels: 317 us -> 298 us
    pallas_call x1, Pallas kernels: 317 us -> 298 us  [by_kernel(): pl.pallas_call(kernel, out_shape=(jax.ShapeDtypeStruct((8, spots), jnp.fl...]
where the time goes in v3:
time: 302 us; the launch traced here: 301 us
  Pallas kernels  298 us (99%)
    pallas_call x1, Pallas kernels, by_kernel(): pl.pallas_call(kernel, out_shape=(jax.ShapeDtypeStruct((8, spots), jnp.fl...  298 us

profile of v3, /device:TPU:0, one launch (start us, length us, event | category | flops | bytes accessed | tf_op | source)
XLA Modules:
  0.0 300.9 jit_solution(7998362437131479331)
XLA Ops:
  0.0 1.3 broadcast_in_dim.2.i_ref
  1.3 0.0 copy-start
  1.3 298.2 %shard_map.55 = (f32[8,128]{1,0:T(8,128)}, bf16[2,4,896,3712]{3,2,1,0:T(8,128)(2,1)}) custom-call(bf16[448,1024]{1,0:T(8,128)(2,1)} %a_ref.1, bf16[448,3712]{1,0:T(8,128)(2,1)} %g_ref.1, f32[1,1024,14848]{2,1,0:T(8,128)} %e_ref.1, s32[8,448]{1,0:T(8,128)} %broadcast_in_dim.2.i_ref), custom_call_target="tpu_custom_call" | custom-call | flops 54492397568 | bytes 167247872 | tf_op jit(solution)/shard_map/pallas_call | solution.py:568
  299.5 0.0 copy-done
  299.5 1.3 divide_bitcast_fusion
Async XLA Ops:
  1.3 298.2 %copy-start = (f32[4]{0:T(128)S(1)}, f32[4]{0:T(128)}, u32[]{:S(2)}) copy-start(f32[4]{0:T(128)} %param.8) | copy-start | bytes 52
